TPU v7x, 32 devices: a whole 2x2x4 slice. The times are simulated.
32 devices in a mesh: groups: 2 (over y), tm: 4 (over z), tile: 2 (over x), arrow: 2 (over core).
Axes of the slice: x: 2, y: 2, z: 4, core: 2. Of those that a mesh axis runs over, the one named last changes fastest.
Arguments:
- forward_blocks: float32 [8, 96, 1024], P(('groups', 'tm'), ('tile', 'arrow')), parts along dimension 0, may hold values from -3 to 3
- arrow_rhs: float32 [192, 64], P(('groups', 'tile', 'arrow')), parts along dimension 0, may hold values from -6 to 6
- diag_inverse: bfloat16 [8, 1024, 1024], P(('groups', 'tm'), None, ('tile', 'arrow')), parts along dimension 0
- lower_coupling: bfloat16 [8, 1024, 1024], P(('groups', 'tm'), None, ('tile', 'arrow')), parts along dimension 0
- arrow_slab: bfloat16 [8, 64, 1024], P(('groups', 'tm'), 'arrow'), parts along dimension 0, may hold values from -0.09375 to 0.09375
- arrow_inverse: float32 [128, 64], P('groups'), parts along dimension 0
- boundary_term: float32 [192, 1024], P(('groups', 'tile', 'arrow')), parts along dimension 0, may hold values from -6 to 6
Outputs:
- solution: float32 [8, 96, 1024], P(('groups', 'tm'), ('tile', 'arrow')), parts along dimension 0
- arrow_solution: float32 [192, 64], P(('groups', 'tile', 'arrow')), parts along dimension 0
There are 2 independent parts, one for each index of `groups`. A program takes and returns all parts, laid end to end along the dimension named above; each array names one. Nothing has to cross between parts.
All inputs are finite; a program needn't handle non-finite values.
Results may differ from a plain program's by a relative error of at most 0.007.
Values may be sent and summed in bfloat16 or wider, within the bound.
A program may use at most 64 MiB of HBM per device.

v0:
```python
import jax
import jax.numpy as jnp
from jax import lax
from jax.sharding import PartitionSpec as P


def from_behind(block, axis, distance):
    devices = range(lax.axis_size(axis))
    route = [(i - distance, i) for i in devices if i - distance in devices]
    return lax.ppermute(block, axis, route)


def shards(
    forward_blocks,
    arrow_rhs,
    diag_inverse,
    lower_coupling,
    arrow_slab,
    arrow_inverse,
    boundary_term,
):
    highest = lax.Precision.HIGHEST
    slab_full = lax.all_gather(arrow_slab, "arrow", axis=1, tiled=True)
    slab_wide = slab_full[0].astype(jnp.float32)
    block_rows = forward_blocks[0]
    local_part = jnp.dot(block_rows, slab_wide.T, precision=highest)
    arrow_sum = lax.psum(local_part, "tm")
    arrow_forward = jnp.dot(arrow_rhs - arrow_sum, arrow_inverse.T, precision=highest)
    arrow_solution = jnp.dot(arrow_forward, arrow_inverse, precision=highest)
    arrow_term = jnp.dot(arrow_solution, slab_wide, precision=highest)
    source_rows = block_rows - arrow_term
    inverse_full, lower_full = (
        lax.all_gather(diag_inverse, ("tile", "arrow"), axis=2, tiled=True),
        lax.all_gather(lower_coupling, ("tile", "arrow"), axis=2, tiled=True),
    )
    coupling = jnp.dot(inverse_full[0], lower_full[0], preferred_element_type=jnp.float32).astype(
        jnp.bfloat16
    )
    coupling_wide = coupling.astype(jnp.float32)
    is_last = (lax.axis_index("tm") == lax.axis_size("tm") - 1).astype(jnp.float32)
    entry_term = is_last * boundary_term

    def one_turn(turn_index, carry_in):
        residual = source_rows - carry_in
        outgoing = jnp.dot(residual, coupling_wide, precision=highest)
        return entry_term + from_behind(outgoing, "tm", -1)

    carry_in = lax.fori_loop(0, lax.axis_size("tm") - 1, one_turn, entry_term)
    residual = source_rows - carry_in
    solution = jnp.dot(
        residual.astype(jnp.bfloat16), inverse_full[0], preferred_element_type=jnp.float32
    )
    return (solution[None], arrow_solution)


def solution(mesh):
    return jax.shard_map(
        shards,
        mesh=mesh,
        in_specs=(
            P(("groups", "tm"), ("tile", "arrow"), None),
            P(("groups", "tile", "arrow"), None),
            P(("groups", "tm"), None, ("tile", "arrow")),
            P(("groups", "tm"), None, ("tile", "arrow")),
            P(("groups", "tm"), "arrow", None),
            P("groups", None),
            P(("groups", "tile", "arrow"), None),
        ),
        out_specs=(
            P(("groups", "tm"), ("tile", "arrow"), None),
            P(("groups", "tile", "arrow"), None),
        ),
        check_vma=False,
    )
```

profile of v0, /device:TPU:0, one launch (start us, length us, event | category | flops | bytes accessed | tf_op | source)
XLA Modules:
  0.0 106.9 jit_solution(2100586051761688842)
XLA Ops:
  7.2 0.7 all-gather.3.cloned.1.call-update
  7.9 0.0 all-gather.5.cloned.1.call-start
  8.0 0.7 all-gather.5.cloned.1.call-update
  8.7 0.9 broadcast_multiply_fusion
  9.6 2.2 %all_gather.9 = bf16[1,64,1024]{2,1,0:T(8,128)(2,1)S(1)} all-gather(bf16[1,32,1024]{2,1,0:T(8,128)(2,1)} %param.13), channel_id=1, replica_groups=mesh['groups'=2,'tm'=4,'tile'=2,'arrow'=2] {'arrow'}, dimensions={1}, use_global_device_ids=true | all-gather | bytes 196608 | tf_op jit(solution)/shard_map/all_gather | solution.py:23
  11.8 1.1 fusion.15
  12.9 20.3 %psum.7 = f32[24,64]{1,0:T(8,128)S(1)} all-reduce(f32[24,64]{1,0:T(8,128)S(1)} %fusion.15), channel_id=1, replica_groups=mesh['groups'=2,'tm'=4,'tile'=2,'arrow'=2] {'tm'}, use_global_device_ids=true, to_apply=%region_0.0 | all-reduce | flops 1536 | bytes 12288 | tf_op jit(solution)/shard_map/psum | solution.py:27
  33.2 0.9 fusion.18
  34.1 0.2 fusion.20
  34.3 0.2 convolution_subtract_fusion
  34.5 0.7 all-gather.3.cloned.1.call-done
  35.1 24.4 %all-gather.5.cloned.1.call-done = bf16[1,1024,1024]{2,1,0:T(8,128)(2,1)} async-done(((bf16[1,1024,256]{2,1,0:T(8,128)(2,1)}), bf16[1,1024,1024]{2,1,0:T(8,128)(2,1)}) %all-gather.5.cloned.1.call-update) | async-done | bytes 2097168 | tf_op jit(solution)/shard_map/all_gather | solution.py:34
  59.6 6.5 %convert_convert_fusion = f32[1024,1024]{1,0:T(8,128)} fusion(bf16[1,1024,1024]{2,1,0:T(8,128)(2,1)} %all-gather.5.cloned.1.call-done, bf16[1,1024,1024]{2,1,0:T(8,128)(2,1)} %all-gather.3.cloned.1.call-done), kind=kOutput, calls=%fused_computation.7 | convolution fusion | flops 2149580800 | bytes 8388608 | tf_op jit(solution)/shard_map/dot_general | solution.py:36
  66.1 32.9 %while.10 = (s32[]{:T(128)}, f32[24,1024]{1,0:T(8,128)S(1)}, f32[24,1024]{1,0:T(8,128)S(1)}, f32[1024,1024]{1,0:T(8,128)}, f32[24,1024]{1,0:T(8,128)S(1)}, /*index=5*/s32[]{:T(128)}) while((s32[]{:T(128)}, f32[24,1024]{1,0:T(8,128)S(1)}, f32[24,1024]{1,0:T(8,128)S(1)}, f32[1024,1024]{1,0:T(8,128)}, f32[24,1024]{1,0:T(8,128)S(1)}, ...), condition=%wide.region_2.0_spmd, body=%wide.region_1.0_spmd.sunk | while | flops 302039040 | bytes 5177453 | solution.py:48
  66.1 4.4 %fusion.31 = f32[24,1024]{1,0:T(8,128)S(1)} fusion(f32[1024,1024]{1,0:T(8,128)} %get-tuple-element.86, f32[24,1024]{1,0:T(8,128)S(1)} %get-tuple-element.85, f32[24,1024]{1,0:T(8,128)S(1)} %get-tuple-element.78), kind=kOutput, calls=%fused_computation.clone.1 | convolution fusion | flops 302014464 | bytes 4489216 | tf_op jit(solution)/shard_map/while/body/eval_jaxpr/dot_general | solution.py:45
  70.5 1.3 %collective-permute-start = (f32[24,1024]{1,0:T(8,128)S(1)}, f32[24,1024]{1,0:T(8,128)S(1)}, u32[]{:S(2)}, u32[]{:S(2)}) collective-permute-start(f32[24,1024]{1,0:T(8,128)S(1)} %fusion.31), channel_id=1, source_target_pairs={{4,0},{8,4},{12,8},{5,1},{9,5},{13,9},{6,2},{10,6},{14,10},{7,3},{... | collective-permute-start | bytes 294920 | tf_op jit(solution)/shard_map/while/body/eval_jaxpr/ppermute | solution.py:10
  71.8 5.6 %collective-permute-done = f32[24,1024]{1,0:T(8,128)S(1)} collective-permute-done((f32[24,1024]{1,0:T(8,128)S(1)}, f32[24,1024]{1,0:T(8,128)S(1)}, u32[]{:S(2)}, u32[]{:S(2)}) %collective-permute-start) | collective-permute-done | bytes 98336 | tf_op jit(solution)/shard_map/while/body/eval_jaxpr/ppermute | solution.py:10
  77.4 4.3 %fusion.31 = f32[24,1024]{1,0:T(8,128)S(1)} fusion(f32[1024,1024]{1,0:T(8,128)} %get-tuple-element.86, f32[24,1024]{1,0:T(8,128)S(1)} %get-tuple-element.85, f32[24,1024]{1,0:T(8,128)S(1)} %get-tuple-element.78), kind=kOutput, calls=%fused_computation.clone.1 | convolution fusion | flops 302014464 | bytes 4489216 | tf_op jit(solution)/shard_map/while/body/eval_jaxpr/dot_general | solution.py:45
  81.7 1.3 %collective-permute-start = (f32[24,1024]{1,0:T(8,128)S(1)}, f32[24,1024]{1,0:T(8,128)S(1)}, u32[]{:S(2)}, u32[]{:S(2)}) collective-permute-start(f32[24,1024]{1,0:T(8,128)S(1)} %fusion.31), channel_id=1, source_target_pairs={{4,0},{8,4},{12,8},{5,1},{9,5},{13,9},{6,2},{10,6},{14,10},{7,3},{... | collective-permute-start | bytes 294920 | tf_op jit(solution)/shard_map/while/body/eval_jaxpr/ppermute | solution.py:10
  83.0 5.2 %collective-permute-done = f32[24,1024]{1,0:T(8,128)S(1)} collective-permute-done((f32[24,1024]{1,0:T(8,128)S(1)}, f32[24,1024]{1,0:T(8,128)S(1)}, u32[]{:S(2)}, u32[]{:S(2)}) %collective-permute-start) | collective-permute-done | bytes 98336 | tf_op jit(solution)/shard_map/while/body/eval_jaxpr/ppermute | solution.py:10
  88.2 4.3 %fusion.31 = f32[24,1024]{1,0:T(8,128)S(1)} fusion(f32[1024,1024]{1,0:T(8,128)} %get-tuple-element.86, f32[24,1024]{1,0:T(8,128)S(1)} %get-tuple-element.85, f32[24,1024]{1,0:T(8,128)S(1)} %get-tuple-element.78), kind=kOutput, calls=%fused_computation.clone.1 | convolution fusion | flops 302014464 | bytes 4489216 | tf_op jit(solution)/shard_map/while/body/eval_jaxpr/dot_general | solution.py:45
  92.5 1.3 %collective-permute-start = (f32[24,1024]{1,0:T(8,128)S(1)}, f32[24,1024]{1,0:T(8,128)S(1)}, u32[]{:S(2)}, u32[]{:S(2)}) collective-permute-start(f32[24,1024]{1,0:T(8,128)S(1)} %fusion.31), channel_id=1, source_target_pairs={{4,0},{8,4},{12,8},{5,1},{9,5},{13,9},{6,2},{10,6},{14,10},{7,3},{... | collective-permute-start | bytes 294920 | tf_op jit(solution)/shard_map/while/body/eval_jaxpr/ppermute | solution.py:10
  93.8 5.2 %collective-permute-done = f32[24,1024]{1,0:T(8,128)S(1)} collective-permute-done((f32[24,1024]{1,0:T(8,128)S(1)}, f32[24,1024]{1,0:T(8,128)S(1)}, u32[]{:S(2)}, u32[]{:S(2)}) %collective-permute-start) | collective-permute-done | bytes 98336 | tf_op jit(solution)/shard_map/while/body/eval_jaxpr/ppermute | solution.py:10
  99.0 1.0 fusion.11
  (13 shorter events, 0.1 us)
Async XLA Ops:
  7.2 26.0 %copy-start = (f32[64,64]{1,0:T(8,128)S(1)}, f32[64,64]{1,0:T(8,128)}, u32[]{:S(2)}) copy-start(f32[64,64]{1,0:T(8,128)} %param.14) | copy-start | bytes 49156
  7.2 27.1 %copy-start.2 = (f32[1,24,1024]{2,1,0:T(8,128)S(1)}, f32[1,24,1024]{2,1,0:T(8,128)}, u32[]{:S(2)}) copy-start(f32[1,24,1024]{2,1,0:T(8,128)} %param.9) | copy-start | bytes 294916
  7.2 28.0 %all-gather.3.cloned.1.call-start = ((), (), s32[]{:S(2)}) async-start(), calls=%async_computation | async-start | bytes 2621440 | tf_op jit(solution)/shard_map/all_gather | solution.py:33
  7.9 51.6 %all-gather.5.cloned.1.call-start = ((), (), s32[]{:S(2)}) async-start(), calls=%async_computation.1 | async-start | bytes 2621440 | tf_op jit(solution)/shard_map/all_gather | solution.py:34
  34.3 31.8 %copy-start.3 = (f32[24,64]{1,0:T(8,128)}, f32[24,64]{1,0:T(8,128)S(1)}, u32[]{:S(2)}) copy-start(f32[24,64]{1,0:T(8,128)S(1)} %fusion.20) | copy-start | bytes 18436
  66.1 33.0 %copy-start.1 = (bf16[1,1024,1024]{2,1,0:T(8,128)(2,1)S(1)}, bf16[1,1024,1024]{2,1,0:T(8,128)(2,1)}, u32[]{:S(2)}) copy-start(bf16[1,1024,1024]{2,1,0:T(8,128)(2,1)} %all-gather.3.cloned.1.call-done) | copy-start | bytes 6291460
  70.5 6.8 %collective-permute-start = (f32[24,1024]{1,0:T(8,128)S(1)}, f32[24,1024]{1,0:T(8,128)S(1)}, u32[]{:S(2)}, u32[]{:S(2)}) collective-permute-start(f32[24,1024]{1,0:T(8,128)S(1)} %fusion.31), channel_id=1, source_target_pairs={{4,0},{8,4},{12,8},{5,1},{9,5},{13,9},{6,2},{10,6},{14,10},{7,3},{... | collective-permute-start | bytes 294920 | tf_op jit(solution)/shard_map/while/body/eval_jaxpr/ppermute | solution.py:10
  81.7 6.5 %collective-permute-start = (f32[24,1024]{1,0:T(8,128)S(1)}, f32[24,1024]{1,0:T(8,128)S(1)}, u32[]{:S(2)}, u32[]{:S(2)}) collective-permute-start(f32[24,1024]{1,0:T(8,128)S(1)} %fusion.31), channel_id=1, source_target_pairs={{4,0},{8,4},{12,8},{5,1},{9,5},{13,9},{6,2},{10,6},{14,10},{7,3},{... | collective-permute-start | bytes 294920 | tf_op jit(solution)/shard_map/while/body/eval_jaxpr/ppermute | solution.py:10
  92.5 6.5 %collective-permute-start = (f32[24,1024]{1,0:T(8,128)S(1)}, f32[24,1024]{1,0:T(8,128)S(1)}, u32[]{:S(2)}, u32[]{:S(2)}) collective-permute-start(f32[24,1024]{1,0:T(8,128)S(1)} %fusion.31), channel_id=1, source_target_pairs={{4,0},{8,4},{12,8},{5,1},{9,5},{13,9},{6,2},{10,6},{14,10},{7,3},{... | collective-permute-start | bytes 294920 | tf_op jit(solution)/shard_map/while/body/eval_jaxpr/ppermute | solution.py:10
Sparse Core Ops, SparseCore 0:
  9.6 25.5 all-gather.2
  36.7 22.8 all-gather.4
where the time goes:
time: 107 us
  waiting for transfers between devices  42.5 us (40%)
  matrix products  22.8 us (21%)
  blocking collectives  22.6 us (21%)
  between operations  14.1 us (13%)
  starting transfers between devices  3.94 us (4%)
    all_gather x1, waiting for transfers between devices, shards(): lax.all_gather(lower_coupling, ('tile', 'arrow'), axis=2, tiled=True)  24.4 us
    psum x1, blocking collectives, shards(): arrow_sum = lax.psum(local_part, 'tm')  20.3 us
    ppermute x3, waiting for transfers between devices, from_behind(): return lax.ppermute(block, axis, route)  16 us
    dot_general x3, matrix products, one_turn(): outgoing = jnp.dot(residual, coupling_wide, precision=highest)  13 us
    dot_general x1, matrix products, shards(): jnp.dot(inverse_full[0], lower_full[0], preferred_element_type=jnp.float32)  6.5 us
    ppermute x3, starting transfers between devices, from_behind(): return lax.ppermute(block, axis, route)  3.86 us
    all_gather x1, blocking collectives, shards(): slab_full = lax.all_gather(arrow_slab, 'arrow', axis=1, tiled=True)  2.21 us
  transfers between devices with their start and end apart: 5, of which 5 were waited for; matrix products, arithmetic and copies ran while one was open for 3% of the time, Pallas kernels for 0%

commit v1 on v0

v1 whole, which is shorter than its diff:
```python
import functools

import jax
import jax.numpy as jnp
from jax import lax
from jax.experimental import pallas as pl
from jax.experimental.pallas import tpu as pltpu
from jax.sharding import PartitionSpec as P

MESH = pl.DeviceIdType.MESH
BF16 = jnp.bfloat16
F32 = jnp.float32
UNROLL_LIMIT = 8


def for_each(first, last, body):
    if last - first <= UNROLL_LIMIT:
        for i in range(first, last):
            body(i)
    else:
        pl.loop(first, last)(body)


def dot(a, b, **kwargs):
    return jnp.dot(a, b, preferred_element_type=F32, **kwargs)


def kernel(
    nt,
    nh,
    fwd_hbm,
    rhs_hbm,
    diag_hbm,
    lower_hbm,
    slab_hbm,
    inv_hbm,
    bound_hbm,
    sol_hbm,
    arrow_hbm,
    fwd,
    rhs,
    inv,
    bound,
    slab,
    diag,
    lower,
    source,
    parts,
    resid,
    accum,
    outgoing,
    incoming,
    finished,
    arrow_out,
    local_sem,
    slab_sem,
    diag_sem,
    source_sems,
    lower_sems,
    relay_sems,
    parts_sems,
    chain_sems,
    out_sems,
):
    t = lax.axis_index("tm")
    h = lax.axis_index("tile")
    core = lax.axis_index("arrow")
    sibling = {"arrow": 1 - core}
    rows = fwd.shape[0]
    width = diag.shape[2]
    wide = 2 * width
    chunks = 2 * nh
    halves = slab.shape[0] // 2
    fixed = slab.shape[0]
    me = t * nh + h
    own_rows = pl.ds(pl.multiple_of(core * halves, halves), halves)

    def tile_rows(j):
        return pl.ds(pl.multiple_of(j * wide, wide), wide)

    def remote(src, dst, send, recv, device):
        return pltpu.make_async_remote_copy(
            src_ref=src,
            dst_ref=dst,
            send_sem=send,
            recv_sem=recv,
            device_id=device,
            device_id_type=MESH,
        )

    def local(src, dst, index):
        return pltpu.make_async_copy(src, dst, local_sem.at[index])

    loads = [
        local(fwd_hbm.at[0], fwd, 0),
        local(slab_hbm.at[0], slab.at[own_rows], 1),
        local(bound_hbm, bound, 2),
        local(rhs_hbm, rhs, 3),
        local(inv_hbm, inv, 4),
        local(diag_hbm.at[0], diag.at[core], 5),
        local(lower_hbm.at[0, tile_rows(h)], lower.at[2 * h + core], 6),
    ]
    for load in loads:
        load.start()

    def coords(index):
        return {"tm": index // nh, "tile": lax.rem(index, nh)}

    def partner(k):
        return lax.rem(me + k, nt * nh)

    def across(k):
        return lax.rem(h + k, nh)

    barrier = pltpu.get_barrier_semaphore()
    pl.semaphore_signal(barrier, inc=1, device_id=sibling, device_id_type=MESH)

    def greet(k):
        pl.semaphore_signal(barrier, inc=1, device_id=coords(partner(k)), device_id_type=MESH)

    for_each(1, nt * nh, greet)
    pl.semaphore_wait(barrier, nt * nh)

    send_slab = remote(
        slab_hbm.at[0], slab.at[own_rows], slab_sem.at[0], slab_sem.at[1], sibling
    )
    send_slab.start()

    loads[0].wait()
    loads[2].wait()
    is_last = (t == nt - 1).astype(F32)
    source[h] = fwd[...] - is_last * bound[...]
    sends = []
    for k in range(1, nh):
        j = across(k)
        copy = remote(
            source.at[h], source.at[h], source_sems.at[0, j], source_sems.at[1, h], {"tile": j}
        )
        copy.start()
        sends.append(copy)
    for k in range(1, nh):
        j = across(k)
        slot = 2 * h + core
        copy = remote(
            lower_hbm.at[0, tile_rows(j)],
            lower.at[slot],
            lower_sems.at[0, j],
            lower_sems.at[1, h],
            {"tile": j},
        )
        copy.start()
        sends.append(copy)
    send_diag = remote(diag_hbm.at[0], diag.at[core], diag_sem.at[0], diag_sem.at[1], sibling)
    send_diag.start()
    relays = [
        remote(
            lower_hbm.at[0, tile_rows(h)],
            lower.at[2 * h + core],
            relay_sems.at[0, h],
            relay_sems.at[1, h],
            sibling,
        )
    ]
    relays[0].start()

    high = fwd[...].astype(BF16)
    low = (fwd[...] - high.astype(F32)).astype(BF16)
    loads[1].wait()
    send_slab.wait()
    contract = (((1,), (1,)), ((), ()))
    part = lax.dot_general(high, slab[...], contract, preferred_element_type=F32)
    part = part + lax.dot_general(low, slab[...], contract, preferred_element_type=F32)
    loads[3].wait()
    parts[me] = (t == 0).astype(F32) * rhs[...] - part

    def part_copy(k):
        other = partner(k)
        return remote(
            parts.at[me], parts.at[me], parts_sems.at[0, other], parts_sems.at[1, me], coords(other)
        )

    for_each(1, nt * nh, lambda k: part_copy(k).start())

    highest = lax.Precision.HIGHEST
    loads[4].wait()
    gram = lax.dot_general(
        inv[...], inv[...], (((0,), (0,)), ((), ())), precision=highest, preferred_element_type=F32
    )

    def part_arrived(k):
        other = partner(k)
        remote(
            parts.at[other],
            parts.at[other],
            parts_sems.at[0, other],
            parts_sems.at[1, other],
            coords(other),
        ).wait_recv()

    for_each(1, nt * nh, part_arrived)
    total = parts[0:nh]
    for i in range(1, nt):
        total = total + parts[i * nh : (i + 1) * nh]
    answer = dot(total.reshape(nh * rows, fixed), gram, precision=highest)
    arrow_out[...] = answer.reshape(nh, rows, fixed)
    write_arrow = pltpu.make_async_copy(arrow_out.at[h], arrow_hbm, local_sem.at[7])
    write_arrow.start()
    answer = answer.astype(BF16)

    for k in range(1, nh):
        j = across(k)
        remote(
            source.at[j], source.at[j], source_sems.at[0, j], source_sems.at[1, j], {"tile": j}
        ).wait_recv()
    for c in range(chunks):
        columns = slice(c * width, (c + 1) * width)
        resid[c] = source[:, :, columns].reshape(nh * rows, width) - dot(answer, slab[:, columns])

    for k in range(1, nh):
        j = across(k)
        slot = lower.at[2 * j + core]
        remote(slot, slot, lower_sems.at[0, j], lower_sems.at[1, j], {"tile": j}).wait_recv()
        copy = remote(slot, slot, relay_sems.at[0, j], relay_sems.at[1, j], sibling)
        copy.start()
        relays.append(copy)

    def lower_arrived():
        loads[6].wait()
        for k in range(nh):
            j = across(k)
            slot = lower.at[2 * j + 1 - core]
            remote(slot, slot, relay_sems.at[0, j], relay_sems.at[1, j], sibling).wait_recv()

    loads[5].wait()
    other_diag = diag.at[1 - core]
    remote(other_diag, other_diag, diag_sem.at[0], diag_sem.at[1], sibling).wait_recv()

    pl.when(t < nt - 1)(lower_arrived)

    accum[...] = jnp.zeros_like(accum)
    for c in reversed(range(chunks)):

        @pl.when(2 * h <= c)
        def _():
            @pl.when(t < nt - 1)
            def _():
                carry = None
                for j in range(nh):
                    slot = incoming.at[j, c]
                    remote(
                        slot,
                        slot,
                        chain_sems.at[0, j, c],
                        chain_sems.at[1, j, c],
                        {"tm": lax.rem(t + 1, nt)},
                    ).wait_recv()
                    term = incoming[j, c].astype(F32)
                    carry = term if carry is None else carry + term
                resid[c] = resid[c] - carry

            rounded = resid[c].astype(BF16)
            for b in range(2):
                accum[b] += dot(rounded, diag[b, c * width : (c + 1) * width, :])

    pl.when(t == nt - 1)(lower_arrived)

    def chain_copy(c, j):
        return remote(
            outgoing.at[c],
            incoming.at[h, c],
            chain_sems.at[0, j, c],
            chain_sems.at[1, h, c],
            {"tm": lax.rem(t + nt - 1, nt), "tile": j},
        )

    @pl.when(t > 0)
    def _():
        first, second = accum[0].astype(BF16), accum[1].astype(BF16)
        for c in reversed(range(chunks)):
            product = dot(first, lower[c, 0:width, :]) + dot(second, lower[c, width:wide, :])
            outgoing[c] = product.astype(BF16)
            for j in range(nh):
                if 2 * j <= c:
                    chain_copy(c, j).start()

    for b in range(2):
        finished[:, :, b * width : (b + 1) * width] = accum[b].reshape(nh, rows, width)
    for k in range(1, nh):
        j = across(k)
        copy = remote(
            finished.at[j],
            sol_hbm.at[0, :, tile_rows(h)],
            out_sems.at[0, j],
            out_sems.at[1, h],
            {"tile": j},
        )
        copy.start()
        sends.append(copy)
    write_own = pltpu.make_async_copy(
        finished.at[h], sol_hbm.at[0, :, tile_rows(h)], local_sem.at[8]
    )
    write_own.start()

    for_each(1, nt * nh, lambda k: part_copy(k).wait_send())
    send_diag.wait_send()
    for copy in sends + relays:
        copy.wait_send()

    @pl.when(t > 0)
    def _():
        for c in range(chunks):
            for j in range(nh):
                if 2 * j <= c:
                    chain_copy(c, j).wait_send()

    write_arrow.wait()
    write_own.wait()
    for k in range(1, nh):
        j = across(k)
        slot = sol_hbm.at[0, :, tile_rows(j)]
        remote(slot, slot, out_sems.at[0, j], out_sems.at[1, j], {"tile": j}).wait_recv()


def solution(mesh):
    nt, nh = mesh.shape["tm"], mesh.shape["tile"]

    def shards(forward, rhs, diag, lower, slab, inverse, boundary):
        _, rows, size = forward.shape
        width = diag.shape[2]
        fixed = rhs.shape[1]
        chunks = 2 * nh
        everything = pl.BlockSpec(memory_space=pl.ANY)
        dma = pltpu.SemaphoreType.DMA
        return pl.pallas_call(
            functools.partial(kernel, nt, nh),
            out_shape=(
                jax.ShapeDtypeStruct(forward.shape, F32),
                jax.ShapeDtypeStruct(rhs.shape, F32),
            ),
            in_specs=[everything] * 7,
            out_specs=(everything, everything),
            scratch_shapes=[
                pltpu.VMEM((rows, size), F32),
                pltpu.VMEM((rows, fixed), F32),
                pltpu.VMEM((fixed, fixed), F32),
                pltpu.VMEM((rows, size), F32),
                pltpu.VMEM((fixed, size), BF16),
                pltpu.VMEM((2, size, width), BF16),
                pltpu.VMEM((chunks, 2 * width, width), BF16),
                pltpu.VMEM((nh, rows, size), F32),
                pltpu.VMEM((nt * nh, rows, fixed), F32),
                pltpu.VMEM((chunks, nh * rows, width), F32),
                pltpu.VMEM((2, nh * rows, width), F32),
                pltpu.VMEM((chunks, nh * rows, width), BF16),
                pltpu.VMEM((nh, chunks, nh * rows, width), BF16),
                pltpu.VMEM((nh, rows, 2 * width), F32),
                pltpu.VMEM((nh, rows, fixed), F32),
                dma((9,)),
                dma((2,)),
                dma((2,)),
                dma((2, nh)),
                dma((2, nh)),
                dma((2, nh)),
                dma((2, nt * nh)),
                dma((2, nh, chunks)),
                dma((2, nh)),
            ],
            compiler_params=pltpu.CompilerParams(
                collective_id=0, has_side_effects=True, vmem_limit_bytes=32 * 1024 * 1024
            ),
        )(forward, rhs, diag, lower, slab, inverse, boundary)

    return jax.shard_map(
        shards,
        mesh=mesh,
        in_specs=(
            P(("groups", "tm"), ("tile", "arrow"), None),
            P(("groups", "tile", "arrow"), None),
            P(("groups", "tm"), None, ("tile", "arrow")),
            P(("groups", "tm"), None, ("tile", "arrow")),
            P(("groups", "tm"), "arrow", None),
            P("groups", None),
            P(("groups", "tile", "arrow"), None),
        ),
        out_specs=(
            P(("groups", "tm"), ("tile", "arrow"), None),
            P(("groups", "tile", "arrow"), None),
        ),
        check_vma=False,
    )
```

time: 107 us -> 45.1 us (0.42)
  waiting for transfers between devices: 42.5 us -> 0 us
  Pallas kernels: 0 us -> 36.6 us
  matrix products: 22.8 us -> 0 us
  blocking collectives: 22.6 us -> 0 us
  between operations: 14.1 us -> 0.66 us
  local copies, waits for them, and re-layouts: 0.04 us -> 7.4 us
  starting transfers between devices: 3.94 us -> 0 us
    pallas_call x0 -> x1, Pallas kernels: none -> 36.6 us  [shards(): pl.pallas_call(functools.partial(kernel, nt, nh), out_shape=(jax.ShapeDty...]
    all_gather x2 -> x0, waiting for transfers between devices: 25.1 us -> none  [the longest x1 24.4 us: shards(): lax.all_gather(lower_coupling, ('tile', 'arrow'), axis=2, tiled=True)]
    dot_general x9 -> x0, matrix products: 22.8 us -> none  [the longest x3 13 us: one_turn(): outgoing = jnp.dot(residual, coupling_wide, precision=highest)]
    psum x1 -> x0, blocking collectives: 20.3 us -> none  [shards(): arrow_sum = lax.psum(local_part, 'tm')]
    ppermute x3 -> x0, waiting for transfers between devices: 16 us -> none  [from_behind(): return lax.ppermute(block, axis, route)]
    unnamed x9 -> x16, local copies, waits for them, and re-layouts: 0.04 us -> 7.4 us
    ppermute x3 -> x0, starting transfers between devices: 3.86 us -> none  [from_behind(): return lax.ppermute(block, axis, route)]
    all_gather x1 -> x0, blocking collectives: 2.21 us -> none  [shards(): slab_full = lax.all_gather(arrow_slab, 'arrow', axis=1, tiled=True)]
  transfers between devices with their start and end apart: 5 -> 0, of which waited for: 5 -> 0; matrix products, arithmetic and copies ran while one was open for 3% -> 0% of each run, Pallas kernels for 0% -> 0%
where the time goes in v1:
time: 45.1 us; the launch traced here: 44.7 us
  Pallas kernels  36.6 us (81%)
  local copies, waits for them, and re-layouts  7.4 us (16%)
  between operations  0.66 us (1%)
    pallas_call x1, Pallas kernels, shards(): pl.pallas_call(functools.partial(kernel, nt, nh), out_shape=(jax.ShapeDty...  36.6 us
    unnamed x16, local copies, waits for them, and re-layouts  7.4 us

profile of v1, /device:TPU:0, one launch (start us, length us, event | category | flops | bytes accessed | tf_op | source)
XLA Modules:
  0.0 44.7 jit_solution(7220342127970016779)
XLA Ops:
  0.6 0.0 copy-start
  0.6 1.0 %copy-done = bf16[1,1024,256]{2,1,0:T(8,128)(2,1)S(1)} copy-done((bf16[1,1024,256]{2,1,0:T(8,128)(2,1)S(1)}, bf16[1,1024,256]{2,1,0:T(8,128)(2,1)}, u32[]{:S(2)}) %copy-start) | copy-done | bytes 524312
  1.7 0.0 copy-start.1
  1.7 1.0 %copy-done.1 = bf16[1,1024,256]{2,1,0:T(8,128)(2,1)S(1)} copy-done((bf16[1,1024,256]{2,1,0:T(8,128)(2,1)S(1)}, bf16[1,1024,256]{2,1,0:T(8,128)(2,1)}, u32[]{:S(2)}) %copy-start.1) | copy-done | bytes 524312
  2.7 0.0 copy-start.2
  2.7 0.9 %copy-done.2 = f32[1,24,1024]{2,1,0:T(8,128)S(1)} copy-done((f32[1,24,1024]{2,1,0:T(8,128)S(1)}, f32[1,24,1024]{2,1,0:T(8,128)}, u32[]{:S(2)}) %copy-start.2) | copy-done | bytes 98328
  3.6 0.0 copy-start.3
  3.6 0.9 %copy-done.3 = f32[24,1024]{1,0:T(8,128)S(1)} copy-done((f32[24,1024]{1,0:T(8,128)S(1)}, f32[24,1024]{1,0:T(8,128)}, u32[]{:S(2)}) %copy-start.3) | copy-done | bytes 98328
  4.5 0.0 copy-start.4
  4.5 0.8 %copy-done.4 = bf16[1,32,1024]{2,1,0:T(8,128)(2,1)S(1)} copy-done((bf16[1,32,1024]{2,1,0:T(8,128)(2,1)S(1)}, bf16[1,32,1024]{2,1,0:T(8,128)(2,1)}, u32[]{:S(2)}) %copy-start.4) | copy-done | bytes 65560
  5.3 0.0 copy-start.5
  5.3 0.8 %copy-done.5 = f32[64,64]{1,0:T(8,128)S(1)} copy-done((f32[64,64]{1,0:T(8,128)S(1)}, f32[64,64]{1,0:T(8,128)}, u32[]{:S(2)}) %copy-start.5) | copy-done | bytes 16408
  6.1 0.0 copy-start.6
  6.1 0.7 %copy-done.6 = f32[24,64]{1,0:T(8,128)S(1)} copy-done((f32[24,64]{1,0:T(8,128)S(1)}, f32[24,64]{1,0:T(8,128)}, u32[]{:S(2)}) %copy-start.6) | copy-done | bytes 6168
  6.8 36.6 %shard_map.86 = (f32[1,24,1024]{2,1,0:T(8,128)S(1)}, f32[24,64]{1,0:T(8,128)S(1)}) custom-call(f32[1,24,1024]{2,1,0:T(8,128)S(1)} %copy-done.2, f32[24,64]{1,0:T(8,128)S(1)} %copy-done.6, bf16[1,1024,256]{2,1,0:T(8,128)(2,1)S(1)} %copy-done, bf16[1,1024,256]{2,1,0:T(8,128)(2,1)S(1)} %copy-done.1, bf16[1,32,1024]{2,1,0:T(8,128)(2,1)S(1)} %copy-done.4, ...), custom_call_target="tpu_custom_call" | custom-call | tf_op jit(solution)/shard_map/pallas_call | solution.py:334
  43.4 0.6 %copy.11 = f32[1,24,1024]{2,1,0:T(8,128)} copy(f32[1,24,1024]{2,1,0:T(8,128)S(1)} %get-tuple-element.4) | data formatting | bytes 196608
  44.1 0.6 %copy.12 = f32[24,64]{1,0:T(8,128)} copy(f32[24,64]{1,0:T(8,128)S(1)} %get-tuple-element.5) | data formatting | bytes 12288
Async XLA Ops:
  0.6 1.0 %copy-start = (bf16[1,1024,256]{2,1,0:T(8,128)(2,1)S(1)}, bf16[1,1024,256]{2,1,0:T(8,128)(2,1)}, u32[]{:S(2)}) copy-start(bf16[1,1024,256]{2,1,0:T(8,128)(2,1)} %diag_hbm.1) | copy-start | bytes 1572868
  1.7 1.0 %copy-start.1 = (bf16[1,1024,256]{2,1,0:T(8,128)(2,1)S(1)}, bf16[1,1024,256]{2,1,0:T(8,128)(2,1)}, u32[]{:S(2)}) copy-start(bf16[1,1024,256]{2,1,0:T(8,128)(2,1)} %lower_hbm.1) | copy-start | bytes 1572868
  2.7 0.9 %copy-start.2 = (f32[1,24,1024]{2,1,0:T(8,128)S(1)}, f32[1,24,1024]{2,1,0:T(8,128)}, u32[]{:S(2)}) copy-start(f32[1,24,1024]{2,1,0:T(8,128)} %fwd_hbm.1) | copy-start | bytes 294916
  3.6 0.9 %copy-start.3 = (f32[24,1024]{1,0:T(8,128)S(1)}, f32[24,1024]{1,0:T(8,128)}, u32[]{:S(2)}) copy-start(f32[24,1024]{1,0:T(8,128)} %bound_hbm.1) | copy-start | bytes 294916
  4.5 0.8 %copy-start.4 = (bf16[1,32,1024]{2,1,0:T(8,128)(2,1)S(1)}, bf16[1,32,1024]{2,1,0:T(8,128)(2,1)}, u32[]{:S(2)}) copy-start(bf16[1,32,1024]{2,1,0:T(8,128)(2,1)} %slab_hbm.1) | copy-start | bytes 196612
  5.3 0.8 %copy-start.5 = (f32[64,64]{1,0:T(8,128)S(1)}, f32[64,64]{1,0:T(8,128)}, u32[]{:S(2)}) copy-start(f32[64,64]{1,0:T(8,128)} %inv_hbm.1) | copy-start | bytes 49156
  6.1 0.7 %copy-start.6 = (f32[24,64]{1,0:T(8,128)S(1)}, f32[24,64]{1,0:T(8,128)}, u32[]{:S(2)}) copy-start(f32[24,64]{1,0:T(8,128)} %rhs_hbm.1) | copy-start | bytes 18436

commit v2 on v1

--- a/solution.py
+++ b/solution.py
@@ -50,6 +50,9 @@
     accum,
     outgoing,
     incoming,
+    row_outgoing,
+    row_incoming,
+    row_accum,
     finished,
     arrow_out,
     local_sem,
@@ -61,6 +64,7 @@
     parts_sems,
     chain_sems,
     out_sems,
+    row_sems,
 ):
     t = lax.axis_index("tm")
     h = lax.axis_index("tile")
@@ -97,11 +101,12 @@
         local(bound_hbm, bound, 2),
         local(rhs_hbm, rhs, 3),
         local(inv_hbm, inv, 4),
-        local(diag_hbm.at[0], diag.at[core], 5),
-        local(lower_hbm.at[0, tile_rows(h)], lower.at[2 * h + core], 6),
+        local(diag_hbm.at[0], diag.at[2 * h + core], 5),
     ]
     for load in loads:
         load.start()
+    load_lower = local(lower_hbm.at[0, tile_rows(h)], lower.at[2 * h + core], 6)
+    pl.when(t > 0)(load_lower.start)
 
     def coords(index):
         return {"tm": index // nh, "tile": lax.rem(index, nh)}
@@ -130,38 +135,50 @@
     loads[2].wait()
     is_last = (t == nt - 1).astype(F32)
     source[h] = fwd[...] - is_last * bound[...]
-    sends = []
-    for k in range(1, nh):
-        j = across(k)
-        copy = remote(
+    mine = 2 * h + core
+
+    def source_copy(j):
+        return remote(
             source.at[h], source.at[h], source_sems.at[0, j], source_sems.at[1, h], {"tile": j}
         )
-        copy.start()
-        sends.append(copy)
-    for k in range(1, nh):
-        j = across(k)
-        slot = 2 * h + core
-        copy = remote(
+
+    def lower_copy(j):
+        return remote(
             lower_hbm.at[0, tile_rows(j)],
-            lower.at[slot],
+            lower.at[mine],
             lower_sems.at[0, j],
             lower_sems.at[1, h],
             {"tile": j},
         )
-        copy.start()
-        sends.append(copy)
-    send_diag = remote(diag_hbm.at[0], diag.at[core], diag_sem.at[0], diag_sem.at[1], sibling)
+
+    def diag_copy(j):
+        return remote(
+            diag_hbm.at[0], diag.at[mine], lower_sems.at[0, j], lower_sems.at[1, h], {"tile": j}
+        )
+
+    own_relay = remote(
+        lower_hbm.at[0, tile_rows(h)],
+        lower.at[mine],
+        relay_sems.at[0, h],
+        relay_sems.at[1, h],
+        sibling,
+    )
+
+    @pl.when(t > 0)
+    def _():
+        for k in range(1, nh):
+            source_copy(across(k)).start()
+        for k in range(1, nh):
+            lower_copy(across(k)).start()
+        own_relay.start()
+
+    @pl.when(t == 0)
+    def _():
+        for k in range(1, nh):
+            diag_copy(across(k)).start()
+
+    send_diag = remote(diag_hbm.at[0], diag.at[mine], diag_sem.at[0], diag_sem.at[1], sibling)
     send_diag.start()
-    relays = [
-        remote(
-            lower_hbm.at[0, tile_rows(h)],
-            lower.at[2 * h + core],
-            relay_sems.at[0, h],
-            relay_sems.at[1, h],
-            sibling,
-        )
-    ]
-    relays[0].start()
 
     high = fwd[...].astype(BF16)
     low = (fwd[...] - high.astype(F32)).astype(BF16)
@@ -203,66 +220,35 @@
         total = total + parts[i * nh : (i + 1) * nh]
     answer = dot(total.reshape(nh * rows, fixed), gram, precision=highest)
     arrow_out[...] = answer.reshape(nh, rows, fixed)
-    write_arrow = pltpu.make_async_copy(arrow_out.at[h], arrow_hbm, local_sem.at[7])
+    write_arrow = pltpu.make_async_copy(arrow_out.at[h], arrow_hbm, local_sem.at[8])
     write_arrow.start()
     answer = answer.astype(BF16)
 
-    for k in range(1, nh):
-        j = across(k)
-        remote(
-            source.at[j], source.at[j], source_sems.at[0, j], source_sems.at[1, j], {"tile": j}
-        ).wait_recv()
-    for c in range(chunks):
-        columns = slice(c * width, (c + 1) * width)
-        resid[c] = source[:, :, columns].reshape(nh * rows, width) - dot(answer, slab[:, columns])
-
-    for k in range(1, nh):
-        j = across(k)
-        slot = lower.at[2 * j + core]
-        remote(slot, slot, lower_sems.at[0, j], lower_sems.at[1, j], {"tile": j}).wait_recv()
-        copy = remote(slot, slot, relay_sems.at[0, j], relay_sems.at[1, j], sibling)
-        copy.start()
-        relays.append(copy)
+    def relay(array, j):
+        slot = array.at[2 * j + core]
+        return remote(slot, slot, relay_sems.at[0, j], relay_sems.at[1, j], sibling)
+
+    def relay_all(array):
+        for k in range(1, nh):
+            j = across(k)
+            slot = array.at[2 * j + core]
+            remote(slot, slot, lower_sems.at[0, j], lower_sems.at[1, j], {"tile": j}).wait_recv()
+            relay(array, j).start()
+
+    def relayed(array, first):
+        for k in range(first, nh):
+            j = across(k)
+            slot = array.at[2 * j + 1 - core]
+            remote(slot, slot, relay_sems.at[0, j], relay_sems.at[1, j], sibling).wait_recv()
+
+    def diag_arrived():
+        loads[5].wait()
+        slot = diag.at[2 * h + 1 - core]
+        remote(slot, slot, diag_sem.at[0], diag_sem.at[1], sibling).wait_recv()
 
     def lower_arrived():
-        loads[6].wait()
-        for k in range(nh):
-            j = across(k)
-            slot = lower.at[2 * j + 1 - core]
-            remote(slot, slot, relay_sems.at[0, j], relay_sems.at[1, j], sibling).wait_recv()
-
-    loads[5].wait()
-    other_diag = diag.at[1 - core]
-    remote(other_diag, other_diag, diag_sem.at[0], diag_sem.at[1], sibling).wait_recv()
-
-    pl.when(t < nt - 1)(lower_arrived)
-
-    accum[...] = jnp.zeros_like(accum)
-    for c in reversed(range(chunks)):
-
-        @pl.when(2 * h <= c)
-        def _():
-            @pl.when(t < nt - 1)
-            def _():
-                carry = None
-                for j in range(nh):
-                    slot = incoming.at[j, c]
-                    remote(
-                        slot,
-                        slot,
-                        chain_sems.at[0, j, c],
-                        chain_sems.at[1, j, c],
-                        {"tm": lax.rem(t + 1, nt)},
-                    ).wait_recv()
-                    term = incoming[j, c].astype(F32)
-                    carry = term if carry is None else carry + term
-                resid[c] = resid[c] - carry
-
-            rounded = resid[c].astype(BF16)
-            for b in range(2):
-                accum[b] += dot(rounded, diag[b, c * width : (c + 1) * width, :])
-
-    pl.when(t == nt - 1)(lower_arrived)
+        load_lower.wait()
+        relayed(lower, 0)
 
     def chain_copy(c, j):
         return remote(
@@ -273,52 +259,169 @@
             {"tm": lax.rem(t + nt - 1, nt), "tile": j},
         )
 
-    @pl.when(t > 0)
-    def _():
-        first, second = accum[0].astype(BF16), accum[1].astype(BF16)
-        for c in reversed(range(chunks)):
-            product = dot(first, lower[c, 0:width, :]) + dot(second, lower[c, width:wide, :])
-            outgoing[c] = product.astype(BF16)
-            for j in range(nh):
-                if 2 * j <= c:
-                    chain_copy(c, j).start()
-
-    for b in range(2):
-        finished[:, :, b * width : (b + 1) * width] = accum[b].reshape(nh, rows, width)
-    for k in range(1, nh):
-        j = across(k)
-        copy = remote(
+    def row_copy(q, j):
+        return remote(
+            row_outgoing.at[q, j],
+            row_incoming.at[h, q],
+            row_sems.at[0, j, q],
+            row_sems.at[1, h, q],
+            {"tm": lax.rem(t + nt - 1, nt), "tile": j},
+        )
+
+    def out_copy(j):
+        return remote(
             finished.at[j],
             sol_hbm.at[0, :, tile_rows(h)],
             out_sems.at[0, j],
             out_sems.at[1, h],
             {"tile": j},
         )
-        copy.start()
-        sends.append(copy)
-    write_own = pltpu.make_async_copy(
-        finished.at[h], sol_hbm.at[0, :, tile_rows(h)], local_sem.at[8]
-    )
-    write_own.start()
+
+    @pl.when(t > 0)
+    def _():
+        for k in range(1, nh):
+            j = across(k)
+            remote(
+                source.at[j], source.at[j], source_sems.at[0, j], source_sems.at[1, j], {"tile": j}
+            ).wait_recv()
+        for c in range(chunks):
+            columns = slice(c * width, (c + 1) * width)
+            resid[c] = source[:, :, columns].reshape(nh * rows, width) - dot(
+                answer, slab[:, columns]
+            )
+        accum[...] = jnp.zeros_like(accum)
+        relay_all(lower)
+        diag_arrived()
+        pl.when(t < nt - 1)(lower_arrived)
+        for c in reversed(range(chunks)):
+
+            @pl.when(2 * h <= c)
+            def _():
+                @pl.when(t < nt - 1)
+                def _():
+                    carry = None
+                    for j in range(nh):
+                        slot = incoming.at[j, c]
+                        remote(
+                            slot,
+                            slot,
+                            chain_sems.at[0, j, c],
+                            chain_sems.at[1, j, c],
+                            {"tm": lax.rem(t + 1, nt)},
+                        ).wait_recv()
+                        term = incoming[j, c].astype(F32)
+                        carry = term if carry is None else carry + term
+                    resid[c] = resid[c] - carry
+
+                rounded = resid[c].astype(BF16)
+                for b in range(2):
+                    accum[b] += dot(rounded, diag[2 * h + b, c * width : (c + 1) * width, :])
+
+        pl.when(t == nt - 1)(lower_arrived)
+        first, second = accum[0].astype(BF16), accum[1].astype(BF16)
+
+        def product(c):
+            return dot(first, lower[c, 0:width, :]) + dot(second, lower[c, width:wide, :])
+
+        @pl.when(t > 1)
+        def _():
+            for c in reversed(range(chunks)):
+                outgoing[c] = product(c).astype(BF16)
+                for j in range(nh):
+                    if 2 * j <= c:
+                        chain_copy(c, j).start()
+
+        @pl.when(t == 1)
+        def _():
+            for q in reversed(range(nh)):
+                left, right = product(2 * q), product(2 * q + 1)
+                for j in range(nh):
+                    mix = slice(j * rows, (j + 1) * rows)
+                    both = jnp.concatenate([left[mix], right[mix]], axis=0)
+                    row_outgoing[q, j] = both.astype(BF16)
+                    row_copy(q, j).start()
+
+        for b in range(2):
+            finished[:, :, b * width : (b + 1) * width] = accum[b].reshape(nh, rows, width)
+        for k in range(1, nh):
+            out_copy(across(k)).start()
+        write_own = pltpu.make_async_copy(
+            finished.at[h], sol_hbm.at[0, :, tile_rows(h)], local_sem.at[7]
+        )
+        write_own.start()
+
+        for k in range(1, nh):
+            j = across(k)
+            source_copy(j).wait_send()
+            lower_copy(j).wait_send()
+            relay(lower, j).wait_send()
+            out_copy(j).wait_send()
+        own_relay.wait_send()
+
+        @pl.when(t > 1)
+        def _():
+            for c in range(chunks):
+                for j in range(nh):
+                    if 2 * j <= c:
+                        chain_copy(c, j).wait_send()
+
+        @pl.when(t == 1)
+        def _():
+            for q in range(nh):
+                for j in range(nh):
+                    row_copy(q, j).wait_send()
+
+        write_own.wait()
+        for k in range(1, nh):
+            j = across(k)
+            slot = sol_hbm.at[0, :, tile_rows(j)]
+            remote(slot, slot, out_sems.at[0, j], out_sems.at[1, j], {"tile": j}).wait_recv()
+
+    @pl.when(t == 0)
+    def _():
+        own_answer = arrow_out[h].astype(BF16)
+        for c in range(chunks):
+            columns = slice(c * width, (c + 1) * width)
+            resid[c, 0:rows, :] = source[h, :, columns] - dot(own_answer, slab[:, columns])
+        row_accum[...] = jnp.zeros_like(row_accum)
+        relay_all(diag)
+        diag_arrived()
+        relayed(diag, 1)
+        for q in reversed(range(nh)):
+            if nt > 1:
+                carry = None
+                for j in range(nh):
+                    slot = row_incoming.at[j, q]
+                    remote(
+                        slot,
+                        slot,
+                        row_sems.at[0, j, q],
+                        row_sems.at[1, j, q],
+                        {"tm": lax.rem(t + 1, nt)},
+                    ).wait_recv()
+                    term = row_incoming[j, q].astype(F32)
+                    carry = term if carry is None else carry + term
+            for c in (2 * q + 1, 2 * q):
+                value = resid[c, 0:rows, :]
+                if nt > 1:
+                    at = (c - 2 * q) * rows
+                    value = value - carry[at : at + rows]
+                rounded = value.astype(BF16)
+                for b in range(c + 1):
+                    row_accum[:, b * width : (b + 1) * width] += dot(
+                        rounded, diag[b, c * width : (c + 1) * width, :]
+                    )
+        write_rows = pltpu.make_async_copy(row_accum, sol_hbm.at[0], local_sem.at[7])
+        write_rows.start()
+        for k in range(1, nh):
+            j = across(k)
+            diag_copy(j).wait_send()
+            relay(diag, j).wait_send()
+        write_rows.wait()
 
     for_each(1, nt * nh, lambda k: part_copy(k).wait_send())
     send_diag.wait_send()
-    for copy in sends + relays:
-        copy.wait_send()
-
-    @pl.when(t > 0)
-    def _():
-        for c in range(chunks):
-            for j in range(nh):
-                if 2 * j <= c:
-                    chain_copy(c, j).wait_send()
-
     write_arrow.wait()
-    write_own.wait()
-    for k in range(1, nh):
-        j = across(k)
-        slot = sol_hbm.at[0, :, tile_rows(j)]
-        remote(slot, slot, out_sems.at[0, j], out_sems.at[1, j], {"tile": j}).wait_recv()
 
 
 def solution(mesh):
@@ -345,7 +448,7 @@
                 pltpu.VMEM((fixed, fixed), F32),
                 pltpu.VMEM((rows, size), F32),
                 pltpu.VMEM((fixed, size), BF16),
-                pltpu.VMEM((2, size, width), BF16),
+                pltpu.VMEM((chunks, size, width), BF16),
                 pltpu.VMEM((chunks, 2 * width, width), BF16),
                 pltpu.VMEM((nh, rows, size), F32),
                 pltpu.VMEM((nt * nh, rows, fixed), F32),
@@ -353,6 +456,9 @@
                 pltpu.VMEM((2, nh * rows, width), F32),
                 pltpu.VMEM((chunks, nh * rows, width), BF16),
                 pltpu.VMEM((nh, chunks, nh * rows, width), BF16),
+                pltpu.VMEM((nh, nh, 2 * rows, width), BF16),
+                pltpu.VMEM((nh, nh, 2 * rows, width), BF16),
+                pltpu.VMEM((rows, size), F32),
                 pltpu.VMEM((nh, rows, 2 * width), F32),
                 pltpu.VMEM((nh, rows, fixed), F32),
                 dma((9,)),
@@ -364,9 +470,10 @@
                 dma((2, nt * nh)),
                 dma((2, nh, chunks)),
                 dma((2, nh)),
+                dma((2, nh, nh)),
             ],
             compiler_params=pltpu.CompilerParams(
-                collective_id=0, has_side_effects=True, vmem_limit_bytes=32 * 1024 * 1024
+                collective_id=0, has_side_effects=True, vmem_limit_bytes=60 * 1024 * 1024
             ),
         )(forward, rhs, diag, lower, slab, inverse, boundary)
 

time: 45.1 us -> 35.8 us (0.79)
  local copies, waits for them, and re-layouts: 7.4 us -> 2.15 us
  Pallas kernels: 36.6 us -> 32.9 us
    unnamed x16 -> x4, local copies, waits for them, and re-layouts: 7.4 us -> 2.15 us
    pallas_call x1, Pallas kernels: 36.6 us -> 32.9 us  [shards(): pl.pallas_call(functools.partial(kernel, nt, nh), out_shape=(jax.ShapeDty...]
where the time goes in v2:
time: 35.8 us; the launch traced here: 35.7 us
  Pallas kernels  32.9 us (92%)
  local copies, waits for them, and re-layouts  2.15 us (6%)
  between operations  0.65 us (2%)
    pallas_call x1, Pallas kernels, shards(): pl.pallas_call(functools.partial(kernel, nt, nh), out_shape=(jax.ShapeDty...  32.9 us
    unnamed x4, local copies, waits for them, and re-layouts  2.15 us

profile of v2, /device:TPU:0, one launch (start us, length us, event | category | flops | bytes accessed | tf_op | source)
XLA Modules:
  0.0 35.7 jit_solution(17899144023384107851)
XLA Ops:
  0.6 32.9 %shard_map.86 = (f32[1,24,1024]{2,1,0:T(8,128)}, f32[24,64]{1,0:T(8,128)}) custom-call(f32[1,24,1024]{2,1,0:T(8,128)} %fwd_hbm.1, f32[24,64]{1,0:T(8,128)} %rhs_hbm.1, bf16[1,1024,256]{2,1,0:T(8,128)(2,1)} %diag_hbm.1, bf16[1,1024,256]{2,1,0:T(8,128)(2,1)} %lower_hbm.1, bf16[1,32,1024]{2,1,0:T(8,128)(2,1)} %slab_hbm.1, f32[64,64]{1,0:T(8,128)} %inv_hbm.1, ...), custom_call_target="tpu_custom_call" | custom-call | tf_op jit(solution)/shard_map/pallas_call | solution.py:437
  33.5 0.0 copy-start
  33.5 1.5 %copy.11 = f32[1,24,1024]{2,1,0:T(8,128)} copy(f32[1,24,1024]{2,1,0:T(8,128)} %get-tuple-element.4) | data formatting | bytes 196608
  35.1 0.0 copy-done
  35.1 0.6 %copy.12 = f32[24,64]{1,0:T(8,128)} copy(f32[24,64]{1,0:T(8,128)S(1)} %copy-done) | data formatting | bytes 12288
Async XLA Ops:
  33.5 1.6 %copy-start = (f32[24,64]{1,0:T(8,128)S(1)}, f32[24,64]{1,0:T(8,128)}, u32[]{:S(2)}) copy-start(f32[24,64]{1,0:T(8,128)} %get-tuple-element.5) | copy-start | bytes 18436

commit v3 on v2

--- a/solution.py
+++ b/solution.py
@@ -45,6 +45,7 @@
     diag,
     lower,
     source,
+    packed,
     parts,
     resid,
     accum,
@@ -71,6 +72,7 @@
     core = lax.axis_index("arrow")
     sibling = {"arrow": 1 - core}
     rows = fwd.shape[0]
+    size = diag.shape[1]
     width = diag.shape[2]
     wide = 2 * width
     chunks = 2 * nh
@@ -131,51 +133,65 @@
     )
     send_slab.start()
 
-    loads[0].wait()
-    loads[2].wait()
     is_last = (t == nt - 1).astype(F32)
-    source[h] = fwd[...] - is_last * bound[...]
     mine = 2 * h + core
 
     def source_copy(j):
         return remote(
-            source.at[h], source.at[h], source_sems.at[0, j], source_sems.at[1, h], {"tile": j}
-        )
-
-    def lower_copy(j):
-        return remote(
-            lower_hbm.at[0, tile_rows(j)],
-            lower.at[mine],
-            lower_sems.at[0, j],
-            lower_sems.at[1, h],
+            packed.at[h], packed.at[h], source_sems.at[0, j], source_sems.at[1, h], {"tile": j}
+        )
+
+    def piece_of(i):
+        return slice(i * width, (i + 1) * width)
+
+    def lower_copy(j, i):
+        return remote(
+            lower_hbm.at[0, pl.ds(pl.multiple_of(j * wide + i * width, width), width)],
+            lower.at[mine, piece_of(i)],
+            lower_sems.at[0, j, i],
+            lower_sems.at[1, h, i],
             {"tile": j},
         )
 
     def diag_copy(j):
         return remote(
-            diag_hbm.at[0], diag.at[mine], lower_sems.at[0, j], lower_sems.at[1, h], {"tile": j}
+            diag_hbm.at[0],
+            diag.at[mine],
+            lower_sems.at[0, j, 0],
+            lower_sems.at[1, h, 0],
+            {"tile": j},
         )
 
     own_relay = remote(
         lower_hbm.at[0, tile_rows(h)],
         lower.at[mine],
-        relay_sems.at[0, h],
-        relay_sems.at[1, h],
+        relay_sems.at[0, h, 0],
+        relay_sems.at[1, h, 0],
         sibling,
     )
 
     @pl.when(t > 0)
     def _():
         for k in range(1, nh):
+            for i in range(2):
+                lower_copy(across(k), i).start()
+        loads[0].wait()
+        loads[2].wait()
+        term = fwd[...] - is_last * bound[...]
+        source[h] = term
+        half = size // 2
+        packed[h] = jnp.concatenate([term[:, :half], term[:, half:]], axis=0).astype(BF16)
+        for k in range(1, nh):
             source_copy(across(k)).start()
-        for k in range(1, nh):
-            lower_copy(across(k)).start()
         own_relay.start()
 
     @pl.when(t == 0)
     def _():
         for k in range(1, nh):
             diag_copy(across(k)).start()
+        loads[0].wait()
+        loads[2].wait()
+        source[h] = fwd[...] - is_last * bound[...]
 
     send_diag = remote(diag_hbm.at[0], diag.at[mine], diag_sem.at[0], diag_sem.at[1], sibling)
     send_diag.start()
@@ -224,22 +240,15 @@
     write_arrow.start()
     answer = answer.astype(BF16)
 
-    def relay(array, j):
-        slot = array.at[2 * j + core]
-        return remote(slot, slot, relay_sems.at[0, j], relay_sems.at[1, j], sibling)
-
-    def relay_all(array):
-        for k in range(1, nh):
-            j = across(k)
-            slot = array.at[2 * j + core]
-            remote(slot, slot, lower_sems.at[0, j], lower_sems.at[1, j], {"tile": j}).wait_recv()
-            relay(array, j).start()
-
-    def relayed(array, first):
-        for k in range(first, nh):
-            j = across(k)
-            slot = array.at[2 * j + 1 - core]
-            remote(slot, slot, relay_sems.at[0, j], relay_sems.at[1, j], sibling).wait_recv()
+    def relay(slot, j, i):
+        return remote(slot, slot, relay_sems.at[0, j, i], relay_sems.at[1, j, i], sibling)
+
+    def lower_piece(j, side, i):
+        return lower.at[2 * j + side, piece_of(i)]
+
+    def relay_on(slot, j, i):
+        remote(slot, slot, lower_sems.at[0, j, i], lower_sems.at[1, j, i], {"tile": j}).wait_recv()
+        relay(slot, j, i).start()
 
     def diag_arrived():
         loads[5].wait()
@@ -248,14 +257,21 @@
 
     def lower_arrived():
         load_lower.wait()
-        relayed(lower, 0)
-
-    def chain_copy(c, j):
-        return remote(
-            outgoing.at[c],
-            incoming.at[h, c],
-            chain_sems.at[0, j, c],
-            chain_sems.at[1, h, c],
+        relay(lower.at[2 * h + 1 - core], h, 0).wait_recv()
+        for k in range(1, nh):
+            j = across(k)
+            for i in range(2):
+                relay(lower_piece(j, 1 - core, i), j, i).wait_recv()
+
+    def pair_of(q):
+        return slice(2 * q, 2 * q + 2)
+
+    def chain_copy(q, j):
+        return remote(
+            outgoing.at[pair_of(q)],
+            incoming.at[h, pair_of(q)],
+            chain_sems.at[0, j, q],
+            chain_sems.at[1, h, q],
             {"tm": lax.rem(t + nt - 1, nt), "tile": j},
         )
 
@@ -282,40 +298,48 @@
         for k in range(1, nh):
             j = across(k)
             remote(
-                source.at[j], source.at[j], source_sems.at[0, j], source_sems.at[1, j], {"tile": j}
+                packed.at[j], packed.at[j], source_sems.at[0, j], source_sems.at[1, j], {"tile": j}
             ).wait_recv()
+            term = packed[j].astype(F32)
+            source[j] = jnp.concatenate([term[:rows], term[rows:]], axis=1)
         for c in range(chunks):
             columns = slice(c * width, (c + 1) * width)
             resid[c] = source[:, :, columns].reshape(nh * rows, width) - dot(
                 answer, slab[:, columns]
             )
         accum[...] = jnp.zeros_like(accum)
-        relay_all(lower)
+        for k in range(1, nh):
+            j = across(k)
+            for i in range(2):
+                relay_on(lower_piece(j, core, i), j, i)
         diag_arrived()
         pl.when(t < nt - 1)(lower_arrived)
-        for c in reversed(range(chunks)):
-
-            @pl.when(2 * h <= c)
+        for q in reversed(range(nh)):
+
+            @pl.when(h <= q)
             def _():
                 @pl.when(t < nt - 1)
                 def _():
-                    carry = None
                     for j in range(nh):
-                        slot = incoming.at[j, c]
+                        slot = incoming.at[j, pair_of(q)]
                         remote(
                             slot,
                             slot,
-                            chain_sems.at[0, j, c],
-                            chain_sems.at[1, j, c],
+                            chain_sems.at[0, j, q],
+                            chain_sems.at[1, j, q],
                             {"tm": lax.rem(t + 1, nt)},
                         ).wait_recv()
-                        term = incoming[j, c].astype(F32)
-                        carry = term if carry is None else carry + term
-                    resid[c] = resid[c] - carry
-
-                rounded = resid[c].astype(BF16)
+                    carry = incoming[0, pair_of(q)].astype(F32)
+                    for j in range(1, nh):
+                        carry = carry + incoming[j, pair_of(q)].astype(F32)
+                    resid[pair_of(q)] = resid[pair_of(q)] - carry
+
                 for b in range(2):
-                    accum[b] += dot(rounded, diag[2 * h + b, c * width : (c + 1) * width, :])
+                    total = accum[b]
+                    for c in (2 * q + 1, 2 * q):
+                        weights = diag[2 * h + b, c * width : (c + 1) * width, :]
+                        total = total + dot(resid[c].astype(BF16), weights)
+                    accum[b] = total
 
         pl.when(t == nt - 1)(lower_arrived)
         first, second = accum[0].astype(BF16), accum[1].astype(BF16)
@@ -325,11 +349,11 @@
 
         @pl.when(t > 1)
         def _():
-            for c in reversed(range(chunks)):
-                outgoing[c] = product(c).astype(BF16)
-                for j in range(nh):
-                    if 2 * j <= c:
-                        chain_copy(c, j).start()
+            for q in reversed(range(nh)):
+                for c in (2 * q + 1, 2 * q):
+                    outgoing[c] = product(c).astype(BF16)
+                for j in range(q + 1):
+                    chain_copy(q, j).start()
 
         @pl.when(t == 1)
         def _():
@@ -353,17 +377,17 @@
         for k in range(1, nh):
             j = across(k)
             source_copy(j).wait_send()
-            lower_copy(j).wait_send()
-            relay(lower, j).wait_send()
+            for i in range(2):
+                lower_copy(j, i).wait_send()
+                relay(lower_piece(j, core, i), j, i).wait_send()
             out_copy(j).wait_send()
         own_relay.wait_send()
 
         @pl.when(t > 1)
         def _():
-            for c in range(chunks):
-                for j in range(nh):
-                    if 2 * j <= c:
-                        chain_copy(c, j).wait_send()
+            for q in range(nh):
+                for j in range(q + 1):
+                    chain_copy(q, j).wait_send()
 
         @pl.when(t == 1)
         def _():
@@ -384,9 +408,13 @@
             columns = slice(c * width, (c + 1) * width)
             resid[c, 0:rows, :] = source[h, :, columns] - dot(own_answer, slab[:, columns])
         row_accum[...] = jnp.zeros_like(row_accum)
-        relay_all(diag)
+        for k in range(1, nh):
+            j = across(k)
+            relay_on(diag.at[2 * j + core], j, 0)
         diag_arrived()
-        relayed(diag, 1)
+        for k in range(1, nh):
+            j = across(k)
+            relay(diag.at[2 * j + 1 - core], j, 0).wait_recv()
         for q in reversed(range(nh)):
             if nt > 1:
                 carry = None
@@ -416,7 +444,7 @@
         for k in range(1, nh):
             j = across(k)
             diag_copy(j).wait_send()
-            relay(diag, j).wait_send()
+            relay(diag.at[2 * j + core], j, 0).wait_send()
         write_rows.wait()
 
     for_each(1, nt * nh, lambda k: part_copy(k).wait_send())
@@ -451,6 +479,7 @@
                 pltpu.VMEM((chunks, size, width), BF16),
                 pltpu.VMEM((chunks, 2 * width, width), BF16),
                 pltpu.VMEM((nh, rows, size), F32),
+                pltpu.VMEM((nh, 2 * rows, size // 2), BF16),
                 pltpu.VMEM((nt * nh, rows, fixed), F32),
                 pltpu.VMEM((chunks, nh * rows, width), F32),
                 pltpu.VMEM((2, nh * rows, width), F32),
@@ -465,10 +494,10 @@
                 dma((2,)),
                 dma((2,)),
                 dma((2, nh)),
-                dma((2, nh)),
-                dma((2, nh)),
+                dma((2, nh, 2)),
+                dma((2, nh, 2)),
                 dma((2, nt * nh)),
-                dma((2, nh, chunks)),
+                dma((2, nh, nh)),
                 dma((2, nh)),
                 dma((2, nh, nh)),
             ],

time: 35.8 us -> 34.7 us (0.969)
  Pallas kernels: 32.9 us -> 31.7 us
    pallas_call x1, Pallas kernels: 32.9 us -> 31.7 us  [shards(): pl.pallas_call(functools.partial(kernel, nt, nh), out_shape=(jax.ShapeDty...]
where the time goes in v3:
time: 34.7 us; the launch traced here: 34.5 us
  Pallas kernels  31.7 us (91%)
  local copies, waits for them, and re-layouts  2.15 us (6%)
  between operations  0.65 us (2%)
    pallas_call x1, Pallas kernels, shards(): pl.pallas_call(functools.partial(kernel, nt, nh), out_shape=(jax.ShapeDty...  31.7 us
    unnamed x4, local copies, waits for them, and re-layouts  2.15 us

profile of v3, /device:TPU:0, one launch (start us, length us, event | category | flops | bytes accessed | tf_op | source)
XLA Modules:
  0.0 34.5 jit_solution(10081928640798670445)
XLA Ops:
  0.6 31.7 %shard_map.86 = (f32[1,24,1024]{2,1,0:T(8,128)}, f32[24,64]{1,0:T(8,128)}) custom-call(f32[1,24,1024]{2,1,0:T(8,128)} %fwd_hbm.1, f32[24,64]{1,0:T(8,128)} %rhs_hbm.1, bf16[1,1024,256]{2,1,0:T(8,128)(2,1)} %diag_hbm.1, bf16[1,1024,256]{2,1,0:T(8,128)(2,1)} %lower_hbm.1, bf16[1,32,1024]{2,1,0:T(8,128)(2,1)} %slab_hbm.1, f32[64,64]{1,0:T(8,128)} %inv_hbm.1, ...), custom_call_target="tpu_custom_call" | custom-call | tf_op jit(solution)/shard_map/pallas_call | solution.py:465
  32.4 0.0 copy-start
  32.4 1.5 %copy.11 = f32[1,24,1024]{2,1,0:T(8,128)} copy(f32[1,24,1024]{2,1,0:T(8,128)} %get-tuple-element.4) | data formatting | bytes 196608
  33.9 0.0 copy-done
  33.9 0.6 %copy.12 = f32[24,64]{1,0:T(8,128)} copy(f32[24,64]{1,0:T(8,128)S(1)} %copy-done) | data formatting | bytes 12288
Async XLA Ops:
  32.4 1.6 %copy-start = (f32[24,64]{1,0:T(8,128)S(1)}, f32[24,64]{1,0:T(8,128)}, u32[]{:S(2)}) copy-start(f32[24,64]{1,0:T(8,128)} %get-tuple-element.5) | copy-start | bytes 18436

commit v4 on v3

--- a/solution.py
+++ b/solution.py
@@ -297,6 +297,10 @@
     def _():
         for k in range(1, nh):
             j = across(k)
+            for i in range(2):
+                relay_on(lower_piece(j, core, i), j, i)
+        for k in range(1, nh):
+            j = across(k)
             remote(
                 packed.at[j], packed.at[j], source_sems.at[0, j], source_sems.at[1, j], {"tile": j}
             ).wait_recv()
@@ -308,10 +312,6 @@
                 answer, slab[:, columns]
             )
         accum[...] = jnp.zeros_like(accum)
-        for k in range(1, nh):
-            j = across(k)
-            for i in range(2):
-                relay_on(lower_piece(j, core, i), j, i)
         diag_arrived()
         pl.when(t < nt - 1)(lower_arrived)
         for q in reversed(range(nh)):

time: 34.7 us -> 34.8 us (level)
  no operation moved by 1% of the time
where the time goes in v4:
time: 34.8 us; the launch traced here: 34.6 us
  Pallas kernels  31.8 us (91%)
  local copies, waits for them, and re-layouts  2.15 us (6%)
  between operations  0.65 us (2%)
    pallas_call x1, Pallas kernels, shards(): pl.pallas_call(functools.partial(kernel, nt, nh), out_shape=(jax.ShapeDty...  31.8 us
    unnamed x4, local copies, waits for them, and re-layouts  2.15 us

profile of v4, /device:TPU:0, one launch (start us, length us, event | category | flops | bytes accessed | tf_op | source)
XLA Modules:
  0.0 34.6 jit_solution(11941810435141874778)
XLA Ops:
  0.6 31.8 %shard_map.86 = (f32[1,24,1024]{2,1,0:T(8,128)}, f32[24,64]{1,0:T(8,128)}) custom-call(f32[1,24,1024]{2,1,0:T(8,128)} %fwd_hbm.1, f32[24,64]{1,0:T(8,128)} %rhs_hbm.1, bf16[1,1024,256]{2,1,0:T(8,128)(2,1)} %diag_hbm.1, bf16[1,1024,256]{2,1,0:T(8,128)(2,1)} %lower_hbm.1, bf16[1,32,1024]{2,1,0:T(8,128)(2,1)} %slab_hbm.1, f32[64,64]{1,0:T(8,128)} %inv_hbm.1, ...), custom_call_target="tpu_custom_call" | custom-call | tf_op jit(solution)/shard_map/pallas_call | solution.py:465
  32.5 0.0 copy-start
  32.5 1.5 %copy.11 = f32[1,24,1024]{2,1,0:T(8,128)} copy(f32[1,24,1024]{2,1,0:T(8,128)} %get-tuple-element.4) | data formatting | bytes 196608
  34.0 0.0 copy-done
  34.0 0.6 %copy.12 = f32[24,64]{1,0:T(8,128)} copy(f32[24,64]{1,0:T(8,128)S(1)} %copy-done) | data formatting | bytes 12288
Async XLA Ops:
  32.5 1.6 %copy-start = (f32[24,64]{1,0:T(8,128)S(1)}, f32[24,64]{1,0:T(8,128)}, u32[]{:S(2)}) copy-start(f32[24,64]{1,0:T(8,128)} %get-tuple-element.5) | copy-start | bytes 18436

commit v5 on v4

--- a/solution.py
+++ b/solution.py
@@ -173,8 +173,7 @@
     @pl.when(t > 0)
     def _():
         for k in range(1, nh):
-            for i in range(2):
-                lower_copy(across(k), i).start()
+            lower_copy(across(k), 0).start()
         loads[0].wait()
         loads[2].wait()
         term = fwd[...] - is_last * bound[...]
@@ -183,6 +182,8 @@
         packed[h] = jnp.concatenate([term[:, :half], term[:, half:]], axis=0).astype(BF16)
         for k in range(1, nh):
             source_copy(across(k)).start()
+        for k in range(1, nh):
+            lower_copy(across(k), 1).start()
         own_relay.start()
 
     @pl.when(t == 0)

time: 34.8 us -> 34.8 us (level)
  no operation moved by 1% of the time
where the time goes in v5:
time: 34.8 us; the launch traced here: 34.6 us
  Pallas kernels  31.8 us (91%)
  local copies, waits for them, and re-layouts  2.15 us (6%)
  between operations  0.65 us (2%)
    pallas_call x1, Pallas kernels, shards(): pl.pallas_call(functools.partial(kernel, nt, nh), out_shape=(jax.ShapeDty...  31.8 us
    unnamed x4, local copies, waits for them, and re-layouts  2.15 us

profile of v5, /device:TPU:0, one launch (start us, length us, event | category | flops | bytes accessed | tf_op | source)
XLA Modules:
  0.0 34.6 jit_solution(14929306524823988129)
XLA Ops:
  0.6 31.8 %shard_map.86 = (f32[1,24,1024]{2,1,0:T(8,128)}, f32[24,64]{1,0:T(8,128)}) custom-call(f32[1,24,1024]{2,1,0:T(8,128)} %fwd_hbm.1, f32[24,64]{1,0:T(8,128)} %rhs_hbm.1, bf16[1,1024,256]{2,1,0:T(8,128)(2,1)} %diag_hbm.1, bf16[1,1024,256]{2,1,0:T(8,128)(2,1)} %lower_hbm.1, bf16[1,32,1024]{2,1,0:T(8,128)(2,1)} %slab_hbm.1, f32[64,64]{1,0:T(8,128)} %inv_hbm.1, ...), custom_call_target="tpu_custom_call" | custom-call | tf_op jit(solution)/shard_map/pallas_call | solution.py:466
  32.5 0.0 copy-start
  32.5 1.5 %copy.11 = f32[1,24,1024]{2,1,0:T(8,128)} copy(f32[1,24,1024]{2,1,0:T(8,128)} %get-tuple-element.4) | data formatting | bytes 196608
  34.0 0.0 copy-done
  34.0 0.6 %copy.12 = f32[24,64]{1,0:T(8,128)} copy(f32[24,64]{1,0:T(8,128)S(1)} %copy-done) | data formatting | bytes 12288
Async XLA Ops:
  32.5 1.6 %copy-start = (f32[24,64]{1,0:T(8,128)S(1)}, f32[24,64]{1,0:T(8,128)}, u32[]{:S(2)}) copy-start(f32[24,64]{1,0:T(8,128)} %get-tuple-element.5) | copy-start | bytes 18436
